TPU v7x, 256 devices: a whole 4x4x8 slice. The times are simulated.
256 devices in a mesh: dp: 32 (over x, z), grp: 8 (over y, core).
Axes of the slice: x: 4, y: 4, z: 8, core: 2. Of those that a mesh axis runs over, the one named last changes fastest.
Arguments:
- q_latent: bfloat16 [4096, 128, 512], P(('grp', 'dp')), parts along dimension 0, may hold values from -60 to 60, as said below
- q_rope: bfloat16 [4096, 64, 128], P(('grp', 'dp')), parts along dimension 0, may hold values from -6 to 6
- cache_latent: bfloat16 [4096, 512, 512], P(('grp', 'dp')), parts along dimension 0, may hold values from -6 to 6
- rope_keys: bfloat16 [4096, 64, 512], P(('grp', 'dp')), parts along dimension 0, may hold values from -6 to 6
- lengths: int32 [4096], P(('grp', 'dp')), parts along dimension 0, may hold values from 1 to 512, as said below
- counts: int32 [256], P(('grp', 'dp')), parts along dimension 0, may hold values from 1 to 16, as said below
- w_uv: bfloat16 [128, 512, 128], P('dp'), may hold values from -0.5 to 0.5
- w_o: bfloat16 [16384, 7168], P('dp'), may hold values from -0.1875 to 0.1875
- residual: bfloat16 [4096, 7168], P(('grp', 'dp')), parts along dimension 0, may hold values from -6 to 6
- norm_gain: bfloat16 [7168], replicated, may hold values from 0.25 to 1.75
Outputs:
- hidden_state: bfloat16 [4096, 7168], P(('grp', 'dp')), parts along dimension 0
- mlp_input: bfloat16 [4096, 7168], P(('grp', 'dp')), parts along dimension 0
There are 8 independent parts, one for each index of `grp`. A program takes and returns all parts, laid end to end along the dimension named above; an argument that names none is the same for every part. Nothing has to cross between parts.
Inputs may be any that keep to these rules, and one draw needn't show every extreme that they name: `lengths`: each slot's context length; in each group some slot holds exactly 512. Lengths differ strongly from device to device. Slots 0 to counts - 1 of a device hold live requests; in each group some device is full. `q_latent`: query entries within -60 to 60.
All inputs are finite; a program needn't handle non-finite values.
Results may differ from a plain program's by a relative error of at most 0.025.
Values may be sent and summed in bfloat16 or wider, within the bound.
A program may use at most 128 MiB of HBM per device.

v0:
```python
import jax
import jax.numpy as jnp
from jax import lax
from jax.sharding import PartitionSpec as P

score_scale = 192.0 ** (-0.5)
norm_eps = 1e-06


def body(
    q_latent, q_rope, cache_latent, rope_keys, lengths, counts, w_uv, w_o, residual, norm_gain
):
    slot_count = q_latent.shape[0]
    context = cache_latent.shape[1]
    scores = jnp.einsum("shk,stk->sht", q_latent, cache_latent, preferred_element_type=jnp.float32)
    scores = scores + jnp.einsum(
        "sjh,sjt->sht", q_rope, rope_keys, preferred_element_type=jnp.float32
    )
    scores = scores * score_scale
    positions = lax.broadcasted_iota(jnp.int32, (slot_count, 1, context), 2)
    visible = positions < lengths[:, None, None]
    scores = jnp.where(visible, scores, jnp.float32(-1e30))
    row_max = jnp.max(scores, axis=2, keepdims=True)
    expos = jnp.where(visible, jnp.exp(scores - row_max), jnp.float32(0.0))
    probs = (expos / jnp.sum(expos, axis=2, keepdims=True)).astype(jnp.bfloat16)
    latent_out = jnp.einsum(
        "sht,stk->shk", probs, cache_latent, preferred_element_type=jnp.float32
    ).astype(jnp.bfloat16)
    routed = lax.all_to_all(latent_out, "dp", split_axis=1, concat_axis=0, tiled=True)
    head_values = jnp.einsum(
        "rhk,hkd->rhd", routed, w_uv, preferred_element_type=jnp.float32
    ).astype(jnp.bfloat16)
    flat_values = head_values.reshape(head_values.shape[0], -1)
    summed = lax.psum_scatter(
        jnp.dot(flat_values, w_o, preferred_element_type=jnp.float32).astype(jnp.bfloat16),
        "dp",
        scatter_dimension=0,
        tiled=True,
    ).astype(jnp.float32)
    live_rows = (jnp.arange(slot_count, dtype=jnp.int32) < counts[0]).astype(jnp.float32)
    hidden_state = (residual.astype(jnp.float32) + live_rows[:, None] * summed).astype(jnp.bfloat16)
    hidden_f = hidden_state.astype(jnp.float32)
    inv_rms = lax.rsqrt(jnp.mean(hidden_f * hidden_f, axis=1, keepdims=True) + norm_eps)
    mlp_input = (hidden_f * inv_rms * norm_gain.astype(jnp.float32)[None, :]).astype(jnp.bfloat16)
    return (hidden_state, mlp_input)


def solution(mesh):
    in_specs = (
        P(("grp", "dp"), None, None),
        P(("grp", "dp"), None, None),
        P(("grp", "dp"), None, None),
        P(("grp", "dp"), None, None),
        P(("grp", "dp")),
        P(("grp", "dp")),
        P("dp", None, None),
        P("dp", None),
        P(("grp", "dp"), None),
        P(),
    )
    out_specs = (P(("grp", "dp"), None), P(("grp", "dp"), None))
    return jax.shard_map(body, mesh=mesh, in_specs=in_specs, out_specs=out_specs, check_vma=False)
```

profile of v0, /device:TPU:32, one launch (start us, length us, event | category | flops | bytes accessed | tf_op | source)
XLA Modules:
  0.0 330.0 jit_solution(602918847030666169)
XLA Ops:
  7.2 0.0 copy-start
  7.2 0.0 reduce-scatter.2.cloned.1.call-start
  7.2 0.9 iota_compare_fusion
  8.1 4.0 %fusion.8 = f32[16,128,512]{2,1,0:T(8,128)} fusion(bf16[16,64,128]{2,1,0:T(8,128)(2,1)} %param.11, bf16[16,64,512]{2,1,0:T(8,128)(2,1)} %param.13), kind=kOutput, calls=%fused_computation.19 | convolution fusion | flops 134217728 | bytes 5505024 | tf_op jit(solution)/shard_map/sjh,sjt->sht/dot_general | solution.py:16
  12.1 0.0 copy-done
  12.1 9.7 %fusion.7 = (f32[16,128]{1,0:T(8,128)S(1)}, f32[16,128,512]{2,1,0:T(8,128)}) fusion(pred[16,512]{1,0:T(8,128)(4,1)S(1)} %iota_compare_fusion, f32[16,128,512]{2,1,0:T(8,128)} %fusion.8, bf16[16,128,512]{2,1,0:T(8,128)(2,1)S(1)} %copy-done, bf16[16,512,512]{2,1,0:T(8,128)(2,1)} %param.12), kind=kOutput, calls=%fused_computation.18 | convolution fusion | flops 1080033792 | bytes 18890752 | tf_op jit(solution)/shard_map/sub | solution.py:24
  21.8 6.1 %fusion.3 = bf16[16,128,512]{2,1,0:T(8,128)(2,1)S(1)} fusion(bf16[16,512,512]{2,1,0:T(8,128)(2,1)} %param.12, f32[16,128,512]{2,1,0:T(8,128)} %get-tuple-element.5, f32[16,128]{1,0:T(8,128)S(1)} %get-tuple-element.4), kind=kOutput, calls=%fused_computation.7 | convolution fusion | flops 1076887552 | bytes 14688256 | tf_op jit(solution)/shard_map/sht,stk->shk/dot_general | solution.py:26
  27.8 0.0 slice-start
  27.8 1.2 copy.14
  29.0 0.0 copy-start.2
  29.0 0.0 slice-start.1
  29.0 62.2 %all_to_all.18 = bf16[16,128,512]{2,0,1:T(8,128)(2,1)S(1)} all-to-all(bf16[16,128,512]{2,0,1:T(8,128)(2,1)S(1)} %copy.14), channel_id=1, replica_groups=mesh['dp'=32,'grp'=8] {'dp'}, dimensions={1} | all-to-all | bytes 4194304 | tf_op jit(solution)/shard_map/all_to_all | solution.py:29
  91.3 0.2 copy.15
  91.5 0.0 copy-done.2
  91.5 0.8 convolution_convert_fusion.1
  92.3 0.0 slice-done
  92.4 0.0 slice-done.1
  92.4 6.2 %convolution_convert_fusion = bf16[512,7168]{1,0:T(8,128)(2,1)} fusion(bf16[512,512]{0,1:T(8,128)(2,1)S(1)} %bitcast.22, bf16[512,7168]{1,0:T(8,128)(2,1)S(1)} %bitcast.21), kind=kOutput, calls=%fused_computation.1 | convolution fusion | flops 3761766400 | bytes 15204352 | tf_op jit(solution)/shard_map/dot_general | solution.py:35
  98.6 0.0 copy-start.4
  98.6 0.0 copy-start.3
  98.6 0.0 reduce-scatter.2.cloned.1.call-update
  99.3 0.0 copy-done.4
  99.3 221.8 %reduce-scatter.2.cloned.1.call-done = bf16[16,7168]{1,0:T(8,128)(2,1)} async-done(((bf16[512,7168]{1,0:T(8,128)(2,1)}), bf16[16,7168]{1,0:T(8,128)(2,1)}) %reduce-scatter.2.cloned.1.call-update) | async-done | bytes 229392 | tf_op jit(solution)/shard_map/reduce_scatter | solution.py:34
  321.1 0.0 copy-done.3
  321.1 1.2 fusion.4
  322.4 0.0 copy-start.1
  322.4 0.8 fusion.6
  323.2 0.0 copy-done.1
  (4 shorter events, 0.0 us)
Async XLA Ops:
  7.2 4.9 %copy-start = (bf16[16,128,512]{2,1,0:T(8,128)(2,1)S(1)}, bf16[16,128,512]{2,1,0:T(8,128)(2,1)}, u32[]{:S(2)}) copy-start(bf16[16,128,512]{2,1,0:T(8,128)(2,1)} %param.10) | copy-start | bytes 6291460
  7.2 314.0 %reduce-scatter.2.cloned.1.call-start = ((), (), s32[]{:S(2)}) async-start(), calls=%async_computation.2 | async-start | bytes 7569408 | tf_op jit(solution)/shard_map/reduce_scatter | solution.py:34
  27.8 64.5 %slice-start = ((s8[7340032]{0:T(1024)(128)(4,1)}), s8[4194304]{0:T(1024)(128)(4,1)S(1)}, s32[]{:S(2)}) async-start(s8[7340032]{0:T(1024)(128)(4,1)} %bitcast.20), calls=%async_computation.3 | async-start | bytes 8388608
  29.0 62.5 %copy-start.2 = (bf16[4,512,128]{2,1,0:T(8,128)(2,1)S(1)}, bf16[4,512,128]{2,1,0:T(8,128)(2,1)}, u32[]{:S(2)}) copy-start(bf16[4,512,128]{2,1,0:T(8,128)(2,1)} %param.16) | copy-start | bytes 1572868
  29.0 63.3 %slice-start.1 = ((s8[7340032]{0:T(1024)(128)(4,1)}), s8[3145728]{0:T(1024)(128)(4,1)S(1)}, s32[]{:S(2)}) async-start(s8[7340032]{0:T(1024)(128)(4,1)} %bitcast.20), calls=%async_computation.4 | async-start | bytes 6291456
  98.6 0.7 copy-start.4
  98.6 222.6 %copy-start.3 = (bf16[16,7168]{1,0:T(8,128)(2,1)S(1)}, bf16[16,7168]{1,0:T(8,128)(2,1)}, u32[]{:S(2)}) copy-start(bf16[16,7168]{1,0:T(8,128)(2,1)} %param.18) | copy-start | bytes 688132
  322.4 0.8 copy-start.1
Sparse Core Ops, SparseCore 0:
  98.7 222.3 reduce-scatter.1
where the time goes:
time: 332 us; the launch traced here: 330 us
  waiting for transfers between devices  222 us (67%)
  blocking collectives  62.2 us (19%)
  matrix products  26.7 us (8%)
  between operations  14.8 us (4%)
    reduce_scatter x1, waiting for transfers between devices, body(): lax.psum_scatter(jnp.dot(flat_values, w_o, preferred_element_type=jnp.flo...  222 us
    all_to_all x1, blocking collectives, body(): lax.all_to_all(latent_out, 'dp', split_axis=1, concat_axis=0, tiled=True)  62.2 us
    sub x1, matrix products, body(): expos = jnp.where(visible, jnp.exp(scores - row_max), jnp.float32(0.0))  9.65 us
  transfers between devices with their start and end apart: 1, of which 1 were waited for; matrix products, arithmetic and copies ran while one was open for 0% of the time, Pallas kernels for 0%

commit v1 on v0

--- a/solution.py
+++ b/solution.py
@@ -1,10 +1,211 @@
 import jax
 import jax.numpy as jnp
 from jax import lax
+from jax.experimental import pallas as pl
+from jax.experimental.pallas import tpu as pltpu
 from jax.sharding import PartitionSpec as P
 
 score_scale = 192.0 ** (-0.5)
 norm_eps = 1e-06
+
+NX, NZ = 4, 8
+SLOTS = 16
+WIDTH = 7168
+DEPTH = 512
+COLS = 256
+XW, ZW = 1024, 768
+MESH = pl.DeviceIdType.MESH
+F32, BF16 = jnp.float32, jnp.bfloat16
+
+
+def hops(size, kind):
+    long, short = size // 2, size // 2 - 1
+    return (long, short) if kind == 0 else (short, long)
+
+
+def project_kernel(
+    hv_ref, wo_ref, res_ref, gain_ref, counts_ref, hid_ref, mlp_ref,
+    wo, px, pz, rx1, rx2, rz1, rz2, acc, load_sem, send_sem, recv_sem,
+):
+    dp, grp = lax.axis_index("dp"), lax.axis_index("grp")
+    x, z = dp // NZ, dp % NZ
+
+    def at_x(step):
+        return (x + step + NX) % NX
+
+    def at_z(step):
+        return (z + step + NZ) % NZ
+
+    def device(dx, dz):
+        return (at_x(dx) * NZ + at_z(dz), grp)
+
+    streams = []
+    for i in range(4):
+        streams.append((True, i, i % 2, i * XW, XW))
+        streams.append((False, i, i % 2, 4 * XW + i * ZW, ZW))
+    loads = []
+    for n, (_, _, _, first, width) in enumerate(streams):
+        load = pltpu.make_async_copy(
+            wo_ref.at[:, pl.ds(first, width)], wo.at[:, pl.ds(first, width)], load_sem.at[n]
+        )
+        load.start()
+        loads.append(load)
+
+    barrier = pltpu.get_barrier_semaphore()
+    for dx, dz in ((1, 0), (-1, 0), (0, 1), (0, -1)):
+        pl.semaphore_signal(barrier, inc=1, device_id=device(dx, dz), device_id_type=MESH)
+    pl.semaphore_wait(barrier, 4)
+
+    copies = {}
+
+    def send(n, phase, way, hop):
+        along_x, i, kind, _, _ = streams[n]
+        axis_x = along_x == (phase == 0)
+        size = NX if axis_x else NZ
+        right, left = hops(size, kind)
+        step = right - hop if way == 0 else hop - left
+        slot = hop if way == 0 else right + hop
+        if along_x:
+            part = px.at[i, at_x(step)] if phase == 0 else px.at[i, x, at_z(step)]
+            land = rx1.at[i, slot] if phase == 0 else rx2.at[i, slot]
+        else:
+            part = pz.at[i, :, at_z(step)] if phase == 0 else pz.at[i, at_x(step), z]
+            land = rz1.at[i, slot] if phase == 0 else rz2.at[i, slot]
+        move = 1 if way == 0 else -1
+        copy = pltpu.make_async_remote_copy(
+            src_ref=part,
+            dst_ref=land,
+            send_sem=send_sem.at[len(copies)],
+            recv_sem=recv_sem.at[len(copies)],
+            device_id=device(move, 0) if axis_x else device(0, move),
+            device_id_type=MESH,
+        )
+        if hop > 0:
+            copies[n, phase, way, hop - 1][0].wait_recv()
+            before = copies[n, phase, way, hop - 1][1]
+            part[...] = (before[...].astype(F32) + part[...].astype(F32)).astype(BF16)
+        copy.start()
+        copies[n, phase, way, hop] = (copy, land)
+
+    def first_hops(n, phase):
+        for way in (0, 1):
+            send(n, phase, way, 0)
+
+    def next_hops(n, phase, hop):
+        along_x, _, kind, _, _ = streams[n]
+        count = hops(NX if along_x == (phase == 0) else NZ, kind)
+        for way in (0, 1):
+            if hop < count[way]:
+                send(n, phase, way, hop)
+
+    def arrivals(n, phase):
+        along_x, _, kind, _, _ = streams[n]
+        count = hops(NX if along_x == (phase == 0) else NZ, kind)
+        total = None
+        for way in (0, 1):
+            copy, land = copies[n, phase, way, count[way] - 1]
+            copy.wait_recv()
+            total = land[...].astype(F32) if total is None else total + land[...].astype(F32)
+        return total
+
+    def turn(n):
+        along_x, i, _, _, _ = streams[n]
+        total = arrivals(n, 0)
+        mine = px.at[i, x] if along_x else pz.at[i, :, z]
+        mine[...] = (mine[...].astype(F32) + total).astype(BF16)
+        first_hops(n, 1)
+
+    live = (
+        lax.broadcasted_iota(jnp.int32, (SLOTS, 1), 0) < counts_ref[0]
+    ).astype(F32)
+
+    def finish(n):
+        along_x, i, _, first, width = streams[n]
+        total = arrivals(n, 1)
+        mine = px.at[i, x, z] if along_x else pz.at[i, x, z]
+        total = total + mine[...].astype(F32)
+        where = pl.ds(first, width)
+        hidden = (res_ref[:, where].astype(F32) + live * total).astype(BF16)
+        hid_ref[:, where] = hidden
+        hidden = hidden.astype(F32)
+        acc[...] += jnp.sum(hidden * hidden, axis=1, keepdims=True)
+
+    acc[...] = jnp.zeros_like(acc)
+    for n, (along_x, i, _, first, width) in enumerate(streams):
+        loads[n].wait()
+        part = px if along_x else pz
+
+        @pl.loop(0, width // COLS)
+        def _(tile):
+            off = pl.multiple_of(tile * COLS, COLS)
+            out = jnp.dot(
+                hv_ref[...], wo[:, pl.ds(first + off, COLS)], preferred_element_type=F32
+            )
+            part[i, :, :, :, pl.ds(off, COLS)] = out.astype(BF16).reshape(NX, NZ, SLOTS, COLS)
+
+        first_hops(n, 0)
+
+    X, Z = (0, 2, 4, 6), (1, 3, 5, 7)
+    plan = [
+        (next_hops, Z[0], 0, 1), (next_hops, X[0], 0, 1), (next_hops, Z[1], 0, 1),
+        (next_hops, Z[2], 0, 1), (next_hops, X[1], 0, 1), (next_hops, Z[3], 0, 1),
+        (next_hops, Z[0], 0, 2), (next_hops, Z[1], 0, 2), (next_hops, X[2], 0, 1),
+        (next_hops, Z[2], 0, 2), (next_hops, Z[3], 0, 2),
+        (turn, X[0]), (next_hops, X[3], 0, 1), (next_hops, Z[0], 0, 3), (next_hops, Z[1], 0, 3),
+        (turn, X[1]), (next_hops, X[0], 1, 1),
+        (next_hops, Z[2], 0, 3), (next_hops, Z[3], 0, 3),
+        (next_hops, X[1], 1, 1), (next_hops, X[0], 1, 2), (turn, Z[0]), (turn, Z[1]),
+        (next_hops, X[1], 1, 2), (next_hops, X[0], 1, 3), (next_hops, X[1], 1, 3),
+        (turn, X[2]), (turn, Z[2]), (turn, Z[3]), (turn, X[3]),
+        (next_hops, Z[0], 1, 1), (next_hops, Z[1], 1, 1),
+        (next_hops, X[2], 1, 1), (next_hops, X[3], 1, 1),
+        (next_hops, Z[2], 1, 1), (next_hops, Z[3], 1, 1),
+        (next_hops, X[2], 1, 2), (next_hops, X[3], 1, 2),
+        (finish, X[0]), (finish, X[1]),
+        (next_hops, X[2], 1, 3), (next_hops, X[3], 1, 3),
+        (finish, Z[0]), (finish, Z[1]), (finish, Z[2]), (finish, Z[3]),
+        (finish, X[2]), (finish, X[3]),
+    ]
+    for act, *rest in plan:
+        act(*rest)
+
+    inv = lax.rsqrt(acc[...] * (1.0 / WIDTH) + norm_eps)
+    mlp_ref[...] = (hid_ref[...].astype(F32) * inv * gain_ref[...].astype(F32)).astype(BF16)
+    for copy, _ in copies.values():
+        copy.wait_send()
+
+
+def project(flat_values, w_o, residual, norm_gain, counts):
+    vmem = pl.BlockSpec(memory_space=pltpu.VMEM)
+    count = 8 * 10
+    return pl.pallas_call(
+        project_kernel,
+        out_shape=[jax.ShapeDtypeStruct((SLOTS, WIDTH), BF16)] * 2,
+        in_specs=[
+            vmem, pl.BlockSpec(memory_space=pl.ANY), vmem, vmem,
+            pl.BlockSpec(memory_space=pltpu.SMEM),
+        ],
+        out_specs=[vmem, vmem],
+        scratch_shapes=[
+            pltpu.VMEM((DEPTH, WIDTH), BF16),
+            pltpu.VMEM((4, NX, NZ, SLOTS, XW), BF16),
+            pltpu.VMEM((4, NX, NZ, SLOTS, ZW), BF16),
+            pltpu.VMEM((4, 3, NZ, SLOTS, XW), BF16),
+            pltpu.VMEM((4, 7, SLOTS, XW), BF16),
+            pltpu.VMEM((4, 7, NX, SLOTS, ZW), BF16),
+            pltpu.VMEM((4, 3, SLOTS, ZW), BF16),
+            pltpu.VMEM((SLOTS, 1), F32),
+            pltpu.SemaphoreType.DMA((8,)),
+            pltpu.SemaphoreType.DMA((count,)),
+            pltpu.SemaphoreType.DMA((count,)),
+        ],
+        compiler_params=pltpu.CompilerParams(
+            collective_id=0, has_side_effects=True, vmem_limit_bytes=48 * 1024 * 1024
+        ),
+        cost_estimate=pl.CostEstimate(
+            flops=2 * 512 * 512 * 7168, bytes_accessed=8 * 1024 * 1024, transcendentals=0
+        ),
+    )(flat_values, w_o, residual, norm_gain.reshape(1, WIDTH), counts)
 
 
 def body(
@@ -31,18 +232,7 @@
         "rhk,hkd->rhd", routed, w_uv, preferred_element_type=jnp.float32
     ).astype(jnp.bfloat16)
     flat_values = head_values.reshape(head_values.shape[0], -1)
-    summed = lax.psum_scatter(
-        jnp.dot(flat_values, w_o, preferred_element_type=jnp.float32).astype(jnp.bfloat16),
-        "dp",
-        scatter_dimension=0,
-        tiled=True,
-    ).astype(jnp.float32)
-    live_rows = (jnp.arange(slot_count, dtype=jnp.int32) < counts[0]).astype(jnp.float32)
-    hidden_state = (residual.astype(jnp.float32) + live_rows[:, None] * summed).astype(jnp.bfloat16)
-    hidden_f = hidden_state.astype(jnp.float32)
-    inv_rms = lax.rsqrt(jnp.mean(hidden_f * hidden_f, axis=1, keepdims=True) + norm_eps)
-    mlp_input = (hidden_f * inv_rms * norm_gain.astype(jnp.float32)[None, :]).astype(jnp.bfloat16)
-    return (hidden_state, mlp_input)
+    return tuple(project(flat_values, w_o, residual, norm_gain, counts))
 
 
 def solution(mesh):

time: 332 us -> 152 us (0.46)
  waiting for transfers between devices: 222 us -> 48.4 us
  Pallas kernels: 0 us -> 63.3 us
  blocking collectives: 62.2 us -> 0 us
  between operations: 14.8 us -> 1.37 us
  starting transfers between devices: 0.04 us -> 11.4 us
  matrix products: 26.7 us -> 20.5 us
  local copies, waits for them, and re-layouts: 1.43 us -> 5.93 us
    reduce_scatter x1 -> x0, waiting for transfers between devices: 222 us -> none  [body(): lax.psum_scatter(jnp.dot(flat_values, w_o, preferred_element_type=jnp.flo...]
    pallas_call x0 -> x1, Pallas kernels: none -> 63.3 us  [project(): pl.pallas_call(project_kernel, out_shape=[jax.ShapeDtypeStruct((SLOTS, WI...]
    all_to_all x1 -> x0, blocking collectives: 62.2 us -> none  [body(): lax.all_to_all(latent_out, 'dp', split_axis=1, concat_axis=0, tiled=True)]
    all_to_all x0 -> x1, waiting for transfers between devices: none -> 48.4 us  [body(): lax.all_to_all(latent_out, 'dp', split_axis=1, concat_axis=0, tiled=True)]
    all_to_all x0 -> x1, starting transfers between devices: none -> 11.4 us  [body(): lax.all_to_all(latent_out, 'dp', split_axis=1, concat_axis=0, tiled=True)]
    dot_general x1 -> x0, matrix products: 6.19 us -> none  [body(): jnp.dot(flat_values, w_o, preferred_element_type=jnp.float32)]
where the time goes in v1:
time: 152 us
  Pallas kernels  63.3 us (42%)
  waiting for transfers between devices  48.4 us (32%)
  matrix products  20.5 us (13%)
  starting transfers between devices  11.4 us (8%)
  local copies, waits for them, and re-layouts  5.93 us (4%)
    pallas_call x1, Pallas kernels, project(): pl.pallas_call(project_kernel, out_shape=[jax.ShapeDtypeStruct((SLOTS, WI...  63.3 us
    all_to_all x1, waiting for transfers between devices, body(): lax.all_to_all(latent_out, 'dp', split_axis=1, concat_axis=0, tiled=True)  48.4 us
    all_to_all x1, starting transfers between devices, body(): lax.all_to_all(latent_out, 'dp', split_axis=1, concat_axis=0, tiled=True)  11.4 us
    sub x1, matrix products, body(): expos = jnp.where(visible, jnp.exp(scores - row_max), jnp.float32(0.0))  9.65 us
    dot_general x1, matrix products, body(): jnp.einsum('sht,stk->shk', probs, cache_latent, preferred_element_type=jn...  6.06 us
    dot_general x1, matrix products, body(): jnp.einsum('sjh,sjt->sht', q_rope, rope_keys, preferred_element_type=jnp....  4 us
  transfers between devices with their start and end apart: 1, of which 1 were waited for; matrix products, arithmetic and copies ran while one was open for 0% of the time, Pallas kernels for 0%

profile of v1, /device:TPU:32, one launch (start us, length us, event | category | flops | bytes accessed | tf_op | source)
XLA Modules:
  0.0 151.8 jit_solution(17495267747130796153)
XLA Ops:
  0.6 0.0 copy-start
  0.6 0.9 iota_compare_fusion
  1.5 4.0 %fusion.5 = f32[16,128,512]{2,1,0:T(8,128)} fusion(bf16[16,64,128]{2,1,0:T(8,128)(2,1)} %param.11, bf16[16,64,512]{2,1,0:T(8,128)(2,1)} %param.13), kind=kOutput, calls=%fused_computation.10 | convolution fusion | flops 134217728 | bytes 5505024 | tf_op jit(solution)/shard_map/sjh,sjt->sht/dot_general | solution.py:217
  5.5 0.0 copy-done
  5.5 9.6 %fusion.4 = (f32[16,128]{1,0:T(8,128)S(1)}, f32[16,128,512]{2,1,0:T(8,128)}) fusion(pred[16,512]{1,0:T(8,128)(4,1)S(1)} %iota_compare_fusion, f32[16,128,512]{2,1,0:T(8,128)} %fusion.5, bf16[16,128,512]{2,1,0:T(8,128)(2,1)S(1)} %copy-done, bf16[16,512,512]{2,1,0:T(8,128)(2,1)} %param.12), kind=kOutput, calls=%fused_computation.9 | convolution fusion | flops 1080033792 | bytes 18890752 | tf_op jit(solution)/shard_map/sub | solution.py:225
  15.2 6.1 %fusion.3 = bf16[16,128,512]{2,1,0:T(8,128)(2,1)S(1)} fusion(bf16[16,512,512]{2,1,0:T(8,128)(2,1)} %param.12, f32[16,128,512]{2,1,0:T(8,128)} %get-tuple-element.3, f32[16,128]{1,0:T(8,128)S(1)} %get-tuple-element.2), kind=kOutput, calls=%fused_computation.6 | convolution fusion | flops 1076887552 | bytes 14688256 | tf_op jit(solution)/shard_map/sht,stk->shk/dot_general | solution.py:227
  21.2 0.0 copy-start.3
  21.3 2.5 %copy.15 = bf16[16,128,512]{2,0,1:T(8,128)(2,1)} copy(bf16[16,128,512]{2,1,0:T(8,128)(2,1)S(1)} %fusion.3) | data formatting | bytes 4194304 | tf_op jit(solution)/shard_map/convert_element_type | solution.py:229
  23.7 0.0 copy-start.2
  23.7 11.4 %all-to-all-start = ((bf16[16,128,512]{2,0,1:T(8,128)(2,1)}), bf16[16,128,512]{2,0,1:T(8,128)(2,1)}, u32[]{:S(2)}, u32[]{:S(2)}) async-start(bf16[16,128,512]{2,0,1:T(8,128)(2,1)} %copy.15), calls=%async_computation | async-start | bytes 4194304 | tf_op jit(solution)/shard_map/all_to_all | solution.py:230
  35.1 0.0 copy-done.3
  35.8 48.4 %all-to-all-done = bf16[16,128,512]{2,0,1:T(8,128)(2,1)} async-done(((bf16[16,128,512]{2,0,1:T(8,128)(2,1)}), bf16[16,128,512]{2,0,1:T(8,128)(2,1)}, u32[]{:S(2)}, u32[]{:S(2)}) %all-to-all-start) | async-done | bytes 2097184 | tf_op jit(solution)/shard_map/all_to_all | solution.py:230
  84.2 0.0 copy-start.1
  84.2 1.8 %copy.16 = bf16[16,32,4,512]{3,0,1,2:T(8,128)(2,1)S(1)} copy(bf16[16,32,4,512]{3,0,2,1:T(8,128)(2,1)} %bitcast) | data formatting | bytes 4194304 | tf_op jit(solution)/shard_map/all_to_all | solution.py:230
  86.1 0.0 copy-done.2
  86.1 0.8 convolution_convert_fusion
  86.9 0.2 copy.20.hv_ref
  87.1 0.0 copy-done.1
  87.1 63.3 %shard_map.113 = (bf16[16,7168]{1,0:T(8,128)(2,1)S(1)}, bf16[16,7168]{1,0:T(8,128)(2,1)S(1)}) custom-call(bf16[512,512]{1,0:T(8,128)(2,1)S(1)} %copy.20.hv_ref, bf16[512,7168]{1,0:T(8,128)(2,1)} %wo_ref.1, bf16[16,7168]{1,0:T(8,128)(2,1)S(1)} %copy-done.1, bf16[1,7168]{1,0:T(2,128)(2,1)S(1)} %reshape.31.gain_ref, s32[1]{0:T(128)S(6)} %copy.23.counts_ref), custom_call_target="tpu_custom_call" | custom-call | flops 3758096384 | bytes 8388608 | tf_op jit(solution)/shard_map/pallas_call | solution.py:181
  150.5 0.7 copy.24
  151.2 0.7 copy.25
  (1 shorter events, 0.0 us)
Async XLA Ops:
  0.6 4.9 %copy-start = (bf16[16,128,512]{2,1,0:T(8,128)(2,1)S(1)}, bf16[16,128,512]{2,1,0:T(8,128)(2,1)}, u32[]{:S(2)}) copy-start(bf16[16,128,512]{2,1,0:T(8,128)(2,1)} %param.10) | copy-start | bytes 6291460
  21.2 13.9 %copy-start.3 = (bf16[7168]{0:T(1024)(128)(2,1)S(1)}, bf16[7168]{0:T(1024)(128)(2,1)}, u32[]{:S(2)}) copy-start(bf16[7168]{0:T(1024)(128)(2,1)} %param.19) | copy-start | bytes 43012
  23.7 62.3 %copy-start.2 = (bf16[4,512,128]{2,1,0:T(8,128)(2,1)S(1)}, bf16[4,512,128]{2,1,0:T(8,128)(2,1)}, u32[]{:S(2)}) copy-start(bf16[4,512,128]{2,1,0:T(8,128)(2,1)} %param.16) | copy-start | bytes 1572868
  23.7 60.5 %all-to-all-start = ((bf16[16,128,512]{2,0,1:T(8,128)(2,1)}), bf16[16,128,512]{2,0,1:T(8,128)(2,1)}, u32[]{:S(2)}, u32[]{:S(2)}) async-start(bf16[16,128,512]{2,0,1:T(8,128)(2,1)} %copy.15), calls=%async_computation | async-start | bytes 4194304 | tf_op jit(solution)/shard_map/all_to_all | solution.py:230
  84.2 2.9 %copy-start.1 = (bf16[16,7168]{1,0:T(8,128)(2,1)S(1)}, bf16[16,7168]{1,0:T(8,128)(2,1)}, u32[]{:S(2)}) copy-start(bf16[16,7168]{1,0:T(8,128)(2,1)} %res_ref.1) | copy-start | bytes 688132

commit v2 on v1

v2 whole, which is shorter than its diff:
```python
import jax
import jax.numpy as jnp
from jax import lax
from jax.experimental import pallas as pl
from jax.experimental.pallas import tpu as pltpu
from jax.sharding import PartitionSpec as P

score_scale = 192.0 ** (-0.5)
log2_e = 1.4426950408889634
norm_eps = 1e-06

NX, NZ = 4, 8
SLOTS = 16
HEADS, LAT, VDIM, ROPE, CTX = 128, 512, 128, 64, 512
OWN = 4
WIDTH = 7168
DEPTH = OWN * VDIM
COLS = 256
GROUP = 2
LANES = 128
XW, ZW = 1024, 768
MESH = pl.DeviceIdType.MESH
F32, BF16 = jnp.float32, jnp.bfloat16


def hops(size, kind):
    long, short = size // 2, size // 2 - 1
    return (long, short) if kind == 0 else (short, long)


def decode_kernel(
    q_hbm, qr_hbm, cache_hbm, rope_hbm, wuv_hbm, wo_hbm, lengths_ref, counts_ref, res_ref, gain_ref,
    hid_ref, mlp_ref,
    q_ref, qr_ref, cache_ref, rope_ref, lat32, lat_out, lat_in, wuv, hv_out, hv,
    wo, px, pz, rx1, rx2, rz1, rz2, acc,
    slot_sem, uv_sem, load_sem,
    ring_send, ring_recv, pair_send, pair_recv, lat_send, lat_recv, hv_send, hv_recv, send_sem, recv_sem,
):
    dp, grp = lax.axis_index("dp"), lax.axis_index("grp")
    x, z = dp // NZ, dp % NZ
    core = grp % 2
    sign = 1 - 2 * core
    sibling = (dp, grp + sign)

    def at_x(step):
        return (x + step + NX) % NX

    def at_z(step):
        return (z + step + NZ) % NZ

    def device(dx, dz):
        return (at_x(dx) * NZ + at_z(dz), grp)

    started = []

    def remote(src, dst, sends, recvs, index, target):
        copy = pltpu.make_async_remote_copy(
            src_ref=src, dst_ref=dst, send_sem=sends.at[index], recv_sem=recvs.at[index],
            device_id=target, device_id_type=MESH,
        )
        copy.start()
        started.append(copy)
        return copy

    barrier = pltpu.get_barrier_semaphore()
    peers = [device(d, 0) for d in range(1, NX)] + [device(0, d) for d in range(1, NZ)] + [sibling]
    for peer in peers:
        pl.semaphore_signal(barrier, inc=1, device_id=peer, device_id_type=MESH)

    uv_load = pltpu.make_async_copy(wuv_hbm, wuv.at[z], uv_sem)
    uv_load.start()

    def slot_loads(group):
        where = pl.ds(group * GROUP, GROUP)
        return [
            pltpu.make_async_copy(hbm.at[where], vmem.at[where], slot_sem.at[n, group])
            for n, (hbm, vmem) in enumerate(
                ((q_hbm, q_ref), (cache_hbm, cache_ref), (qr_hbm, qr_ref), (rope_hbm, rope_ref))
            )
        ]

    for group in range(SLOTS // GROUP):
        for load in slot_loads(group):
            load.start()

    streams = []
    for i in range(4):
        streams.append((True, i, i % 2, i * XW, XW))
        streams.append((False, i, i % 2, 4 * XW + i * ZW, ZW))
    loads = []
    for n, (_, _, _, first, width) in enumerate(streams):
        load = pltpu.make_async_copy(
            wo_hbm.at[:, pl.ds(first, width)], wo.at[:, pl.ds(first, width)], load_sem.at[n]
        )
        load.start()
        loads.append(load)

    position = lax.broadcasted_iota(jnp.int32, (1, CTX), 1)

    def attend(slot):
        scores = lax.dot_general(
            q_ref[slot], cache_ref[slot], (((1,), (1,)), ((), ())), preferred_element_type=F32
        )
        scores += lax.dot_general(
            qr_ref[slot], rope_ref[slot], (((0,), (0,)), ((), ())), preferred_element_type=F32
        )
        scores = jnp.where(position < lengths_ref[slot], scores, -1e30)
        top = jnp.max(scores, axis=1, keepdims=True)
        expos = jnp.exp2((scores - top) * (score_scale * log2_e))
        probs = (expos * (1.0 / jnp.sum(expos, axis=1, keepdims=True))).astype(BF16)
        rows = pl.ds(pl.multiple_of(slot * HEADS, HEADS), HEADS)
        latents = jnp.dot(probs, cache_ref[slot], preferred_element_type=F32)
        for k in range(LAT // LANES):
            lat32[k, rows, :] = latents[:, k * LANES : (k + 1) * LANES]

    def attend_groups(first, last):
        @pl.loop(first, last)
        def _(group):
            for load in slot_loads(group):
                load.wait()
            for j in range(GROUP):
                attend(group * GROUP + j)

    ring_hops = (NZ // 2, NZ // 2 - 1)
    ring, pair = {}, {}

    def origin(way, hop):
        return at_z(hop * (-sign if way == 0 else sign))

    def ring_send_hop(way, hop):
        to = (x * NZ + at_z(sign if way == 0 else -sign), grp)
        for k in range(2):
            piece = wuv.at[origin(way, hop), core * 2 + k]
            index = (way * 4 + hop) * 2 + k
            ring[way, hop, k] = remote(piece, piece, ring_send, ring_recv, index, to)

    def ring_step(hop):
        for way in (0, 1):
            if hop >= ring_hops[way]:
                continue
            for k in range(2):
                ring[way, hop, k].wait_recv()
            if hop + 1 < ring_hops[way]:
                ring_send_hop(way, hop + 1)
            for k in range(2):
                piece = wuv.at[origin(way, hop + 1), core * 2 + k]
                index = (way * 4 + hop) * 2 + k
                pair[way, hop, k] = remote(piece, piece, pair_send, pair_recv, index, sibling)

    attend_groups(0, 1)
    pl.semaphore_wait(barrier, len(peers))
    uv_load.wait()
    ring_send_hop(0, 0)
    ring_send_hop(1, 0)
    attend_groups(1, 6)
    ring_step(0)
    attend_groups(6, 8)

    order = (0, 1, -1, 2, -2, 3, -3, 4)
    moved = {}
    for n, offset in enumerate(order):
        to_z = at_z(offset * sign)
        for step in range(NX):
            to_x = at_x(step)

            @pl.loop(0, OWN, unroll=True)
            def _(j):
                head = (to_x * NZ + to_z) * OWN + j
                for k in range(LAT // LANES):
                    rows = lat32[k, pl.ds(head, SLOTS, stride=HEADS), :].astype(BF16)
                    where = pl.ds(k * LANES, LANES)
                    if step == 0:
                        lat_in[n, j, x, :, where] = rows
                    else:
                        lat_out[step - 1, n, j, :, where] = rows

            if step > 0:
                moved[n, step] = remote(
                    lat_out.at[step - 1, n], lat_in.at[n, :, x], lat_send, lat_recv,
                    (step - 1) * NZ + n, device(step, 0),
                )
        if n == 3:
            ring_step(1)

    valued = []
    for n, offset in enumerate(order):
        if n == 2:
            ring_step(2)
        if n == 4:
            ring_step(3)
        to_z = at_z(offset * sign)
        if n > 0:
            hop = abs(offset) - 1
            for k in range(2):
                pair[(1 if offset < 0 else 0), hop, k].wait_recv()
        for step in range(1, NX):
            moved[n, step].wait_recv()
        out = hv.at[z] if n == 0 else hv_out.at[n - 1]
        for j in range(OWN):
            rows = lat_in[n, j].reshape(NX * SLOTS, LAT)
            value = jnp.dot(rows, wuv[to_z, j], preferred_element_type=F32)
            out[:, pl.ds(j * VDIM, VDIM)] = value.astype(BF16)
        if n > 0:
            valued.append(remote(out, hv.at[z], hv_send, hv_recv, n - 1, device(0, offset * sign)))
    for copy in valued:
        copy.wait_recv()

    copies = {}

    def send(n, phase, way, hop):
        along_x, i, kind, _, _ = streams[n]
        axis_x = along_x == (phase == 0)
        size = NX if axis_x else NZ
        right, left = hops(size, kind)
        step = right - hop if way == 0 else hop - left
        slot = hop if way == 0 else right + hop
        if along_x:
            part = px.at[i, :, at_x(step)] if phase == 0 else px.at[i, at_z(step), x]
            land = rx1.at[i, slot] if phase == 0 else rx2.at[i, slot]
        else:
            part = pz.at[i, at_z(step)] if phase == 0 else pz.at[i, z, at_x(step)]
            land = rz1.at[i, slot] if phase == 0 else rz2.at[i, slot]
        move = 1 if way == 0 else -1
        if hop > 0:
            copies[n, phase, way, hop - 1][0].wait_recv()
            before = copies[n, phase, way, hop - 1][1]
            part[...] = (before[...].astype(F32) + part[...].astype(F32)).astype(BF16)
        copy = remote(
            part, land, send_sem, recv_sem, len(copies),
            device(move, 0) if axis_x else device(0, move),
        )
        copies[n, phase, way, hop] = (copy, land)

    def first_hops(n, phase):
        for way in (0, 1):
            send(n, phase, way, 0)

    def next_hops(n, phase, hop):
        along_x, _, kind, _, _ = streams[n]
        count = hops(NX if along_x == (phase == 0) else NZ, kind)
        for way in (0, 1):
            if hop < count[way]:
                send(n, phase, way, hop)

    def arrivals(n, phase):
        along_x, _, kind, _, _ = streams[n]
        count = hops(NX if along_x == (phase == 0) else NZ, kind)
        total = None
        for way in (0, 1):
            copy, land = copies[n, phase, way, count[way] - 1]
            copy.wait_recv()
            total = land[...].astype(F32) if total is None else total + land[...].astype(F32)
        return total

    def turn(n):
        along_x, i, _, _, _ = streams[n]
        total = arrivals(n, 0)
        mine = px.at[i, :, x] if along_x else pz.at[i, z]
        mine[...] = (mine[...].astype(F32) + total).astype(BF16)
        first_hops(n, 1)

    live = (
        lax.broadcasted_iota(jnp.int32, (SLOTS, 1), 0) < counts_ref[0]
    ).astype(F32)

    def finish(n):
        along_x, i, _, first, width = streams[n]
        total = arrivals(n, 1)
        mine = px.at[i, z, x] if along_x else pz.at[i, z, x]
        total = total + mine[...].astype(F32)
        where = pl.ds(first, width)
        hidden = (res_ref[:, where].astype(F32) + live * total).astype(BF16)
        hid_ref[:, where] = hidden
        hidden = hidden.astype(F32)
        acc[...] += jnp.sum(hidden * hidden, axis=1, keepdims=True)

    acc[...] = jnp.zeros_like(acc)
    for n, (along_x, i, _, first, width) in enumerate(streams):
        loads[n].wait()
        part = px if along_x else pz

        @pl.loop(0, width // COLS)
        def _(tile):
            off = pl.multiple_of(tile * COLS, COLS)
            out = jnp.dot(
                hv[...].reshape(NX * NZ * SLOTS, DEPTH), wo[:, pl.ds(first + off, COLS)], preferred_element_type=F32
            )
            part[i, :, :, :, pl.ds(off, COLS)] = out.astype(BF16).reshape(NZ, NX, SLOTS, COLS)

        first_hops(n, 0)

    X, Z = (0, 2, 4, 6), (1, 3, 5, 7)
    plan = [
        (next_hops, Z[0], 0, 1), (next_hops, X[0], 0, 1), (next_hops, Z[1], 0, 1),
        (next_hops, Z[2], 0, 1), (next_hops, X[1], 0, 1), (next_hops, Z[3], 0, 1),
        (next_hops, Z[0], 0, 2), (next_hops, Z[1], 0, 2), (next_hops, X[2], 0, 1),
        (next_hops, Z[2], 0, 2), (next_hops, Z[3], 0, 2),
        (turn, X[0]), (next_hops, X[3], 0, 1), (next_hops, Z[0], 0, 3), (next_hops, Z[1], 0, 3),
        (turn, X[1]), (next_hops, X[0], 1, 1),
        (next_hops, Z[2], 0, 3), (next_hops, Z[3], 0, 3),
        (next_hops, X[1], 1, 1), (next_hops, X[0], 1, 2), (turn, Z[0]), (turn, Z[1]),
        (next_hops, X[1], 1, 2), (next_hops, X[0], 1, 3), (next_hops, X[1], 1, 3),
        (turn, X[2]), (turn, Z[2]), (turn, Z[3]), (turn, X[3]),
        (next_hops, Z[0], 1, 1), (next_hops, Z[1], 1, 1),
        (next_hops, X[2], 1, 1), (next_hops, X[3], 1, 1),
        (next_hops, Z[2], 1, 1), (next_hops, Z[3], 1, 1),
        (next_hops, X[2], 1, 2), (next_hops, X[3], 1, 2),
        (finish, X[0]), (finish, X[1]),
        (next_hops, X[2], 1, 3), (next_hops, X[3], 1, 3),
        (finish, Z[0]), (finish, Z[1]), (finish, Z[2]), (finish, Z[3]),
        (finish, X[2]), (finish, X[3]),
    ]
    for act, *rest in plan:
        act(*rest)

    inv = lax.rsqrt(acc[...] * (1.0 / WIDTH) + norm_eps)
    mlp_ref[...] = (hid_ref[...].astype(F32) * inv * gain_ref[...].astype(F32)).astype(BF16)
    for copy in started:
        copy.wait_send()


def body(
    q_latent, q_rope, cache_latent, rope_keys, lengths, counts, w_uv, w_o, residual, norm_gain
):
    vmem = pl.BlockSpec(memory_space=pltpu.VMEM)
    smem = pl.BlockSpec(memory_space=pltpu.SMEM)
    hbm = pl.BlockSpec(memory_space=pl.ANY)
    dma = pltpu.SemaphoreType.DMA
    rows = NX * NZ * SLOTS
    outs = pl.pallas_call(
        decode_kernel,
        out_shape=[jax.ShapeDtypeStruct((SLOTS, WIDTH), BF16)] * 2,
        in_specs=[hbm] * 6 + [smem] * 2 + [vmem] * 2,
        out_specs=[vmem, vmem],
        scratch_shapes=[
            pltpu.VMEM((SLOTS, HEADS, LAT), BF16),
            pltpu.VMEM((SLOTS, ROPE, HEADS), BF16),
            pltpu.VMEM((SLOTS, CTX, LAT), BF16),
            pltpu.VMEM((SLOTS, ROPE, CTX), BF16),
            pltpu.VMEM((LAT // LANES, SLOTS * HEADS, LANES), F32),
            pltpu.VMEM((NX - 1, NZ, OWN, SLOTS, LAT), BF16),
            pltpu.VMEM((NZ, OWN, NX, SLOTS, LAT), BF16),
            pltpu.VMEM((NZ, OWN, LAT, VDIM), BF16),
            pltpu.VMEM((NZ - 1, NX * SLOTS, DEPTH), BF16),
            pltpu.VMEM((NZ, NX * SLOTS, DEPTH), BF16),
            pltpu.VMEM((DEPTH, WIDTH), BF16),
            pltpu.VMEM((4, NZ, NX, SLOTS, XW), BF16),
            pltpu.VMEM((4, NZ, NX, SLOTS, ZW), BF16),
            pltpu.VMEM((4, 3, NZ, SLOTS, XW), BF16),
            pltpu.VMEM((4, 7, SLOTS, XW), BF16),
            pltpu.VMEM((4, 7, NX, SLOTS, ZW), BF16),
            pltpu.VMEM((4, 3, SLOTS, ZW), BF16),
            pltpu.VMEM((SLOTS, 1), F32),
            dma((4, SLOTS // GROUP)), dma, dma((8,)),
            dma((16,)), dma((16,)), dma((16,)), dma((16,)),
            dma((24,)), dma((24,)), dma((7,)), dma((7,)), dma((80,)), dma((80,)),
        ],
        compiler_params=pltpu.CompilerParams(
            collective_id=0, has_side_effects=True, vmem_limit_bytes=56 * 1024 * 1024
        ),
        cost_estimate=pl.CostEstimate(
            flops=2 * rows * DEPTH * WIDTH, bytes_accessed=20 * 1024 * 1024, transcendentals=0
        ),
    )(
        q_latent, q_rope, cache_latent, rope_keys, w_uv, w_o, lengths, counts, residual,
        norm_gain.reshape(1, WIDTH),
    )
    return tuple(outs)


def solution(mesh):
    in_specs = (
        P(("grp", "dp"), None, None),
        P(("grp", "dp"), None, None),
        P(("grp", "dp"), None, None),
        P(("grp", "dp"), None, None),
        P(("grp", "dp")),
        P(("grp", "dp")),
        P("dp", None, None),
        P("dp", None),
        P(("grp", "dp"), None),
        P(),
    )
    out_specs = (P(("grp", "dp"), None), P(("grp", "dp"), None))
    return jax.shard_map(body, mesh=mesh, in_specs=in_specs, out_specs=out_specs, check_vma=False)
```

time: 152 us -> 122 us (0.80)
  Pallas kernels: 63.3 us -> 115 us
  waiting for transfers between devices: 48.4 us -> 0 us
  matrix products: 20.5 us -> 0 us
  starting transfers between devices: 11.4 us -> 0 us
    pallas_call x1, Pallas kernels: 63.3 us -> 115 us  [body(): pl.pallas_call(decode_kernel, out_shape=[jax.ShapeDtypeStruct((SLOTS, WID...]
    all_to_all x1 -> x0, waiting for transfers between devices: 48.4 us -> none  [body(): lax.all_to_all(latent_out, 'dp', split_axis=1, concat_axis=0, tiled=True)]
    all_to_all x1 -> x0, starting transfers between devices: 11.4 us -> none  [body(): lax.all_to_all(latent_out, 'dp', split_axis=1, concat_axis=0, tiled=True)]
    dot_general x3 -> x0, matrix products: 10.9 us -> none  [the longest x1 6.06 us: body(): jnp.einsum('sht,stk->shk', probs, cache_latent, preferred_element_type=jn...]
    sub x1 -> x0, matrix products: 9.65 us -> none  [body(): expos = jnp.where(visible, jnp.exp(scores - row_max), jnp.float32(0.0))]
    convert_element_type x1 -> x0, local copies, waits for them, and re-layouts: 2.47 us -> none  [body(): latent_out = jnp.einsum('sht,stk->shk', probs, cache_latent, preferred_el...]
    unnamed x10 -> x2, local copies, waits for them, and re-layouts: 1.4 us -> 3.28 us
    all_to_all x1 -> x0, local copies, waits for them, and re-layouts: 1.82 us -> none  [body(): lax.all_to_all(latent_out, 'dp', split_axis=1, concat_axis=0, tiled=True)]
  transfers between devices with their start and end apart: 1 -> 0, of which waited for: 1 -> 0; matrix products, arithmetic and copies ran while one was open for 0% -> 0% of each run, Pallas kernels for 0% -> 0%
where the time goes in v2:
time: 122 us; the launch traced here: 121 us
  Pallas kernels  115 us (94%)
  local copies, waits for them, and re-layouts  4.62 us (4%)
  between operations  1.29 us (1%)
    pallas_call x1, Pallas kernels, body(): pl.pallas_call(decode_kernel, out_shape=[jax.ShapeDtypeStruct((SLOTS, WID...  115 us
    unnamed x2, local copies, waits for them, and re-layouts  3.28 us

profile of v2, /device:TPU:32, one launch (start us, length us, event | category | flops | bytes accessed | tf_op | source)
XLA Modules:
  0.0 120.5 jit_solution(12433223294586538878)
XLA Ops:
  1.3 1.3 %reshape.7.gain_ref = bf16[1,7168]{1,0:T(2,128)(2,1)} reshape(bf16[7168]{0:T(1024)(128)(2,1)} %param.19) | data formatting | bytes 28672 | tf_op jit(solution)/shard_map/reshape | solution.py:366
  2.6 114.6 %shard_map.113 = (bf16[16,7168]{1,0:T(8,128)(2,1)}, bf16[16,7168]{1,0:T(8,128)(2,1)}) custom-call(bf16[16,128,512]{2,1,0:T(8,128)(2,1)} %q_hbm.1, bf16[16,64,128]{2,1,0:T(8,128)(2,1)} %qr_hbm.1, bf16[16,512,512]{2,1,0:T(8,128)(2,1)} %cache_hbm.1, bf16[16,64,512]{2,1,0:T(8,128)(2,1)} %rope_hbm.1, bf16[4,512,128]{2,1,0:T(8,128)(2,1)} %wuv_hbm.1, ...), custom_call_target="tpu_custom_call" | custom-call | flops 3758096384 | bytes 20971520 | tf_op jit(solution)/shard_map/pallas_call | solution.py:330
  117.2 1.6 %copy.15 = bf16[16,7168]{1,0:T(8,128)(2,1)} copy(bf16[16,7168]{1,0:T(8,128)(2,1)} %get-tuple-element.4) | data formatting | bytes 458752
  118.9 1.6 %copy.16 = bf16[16,7168]{1,0:T(8,128)(2,1)} copy(bf16[16,7168]{1,0:T(8,128)(2,1)} %get-tuple-element.5) | data formatting | bytes 458752

commit v3 on v2

--- a/solution.py
+++ b/solution.py
@@ -67,8 +67,14 @@
     for peer in peers:
         pl.semaphore_signal(barrier, inc=1, device_id=peer, device_id_type=MESH)
 
-    uv_load = pltpu.make_async_copy(wuv_hbm, wuv.at[z], uv_sem)
-    uv_load.start()
+    uv_loads = [
+        pltpu.make_async_copy(
+            wuv_hbm.at[j], wuv.at[z, j // 2, :, pl.ds(j % 2 * VDIM, VDIM)], uv_sem.at[j]
+        )
+        for j in range(OWN)
+    ]
+    for load in uv_loads:
+        load.start()
 
     def slot_loads(group):
         where = pl.ds(group * GROUP, GROUP)
@@ -124,84 +130,112 @@
     ring_hops = (NZ // 2, NZ // 2 - 1)
     ring, pair = {}, {}
 
-    def origin(way, hop):
-        return at_z(hop * (-sign if way == 0 else sign))
-
-    def ring_send_hop(way, hop):
+    def uv_piece(way, hop, k):
+        origin = at_z(hop * (-sign if way == 0 else sign))
+        return wuv.at[origin, core, pl.ds(k * (LAT // 2), LAT // 2)]
+
+    def ring_hop(way, hop, k):
         to = (x * NZ + at_z(sign if way == 0 else -sign), grp)
-        for k in range(2):
-            piece = wuv.at[origin(way, hop), core * 2 + k]
-            index = (way * 4 + hop) * 2 + k
-            ring[way, hop, k] = remote(piece, piece, ring_send, ring_recv, index, to)
-
-    def ring_step(hop):
+        piece = uv_piece(way, hop, k)
+        index = (way * 4 + hop) * 2 + k
+        ring[way, hop, k] = remote(piece, piece, ring_send, ring_recv, index, to)
+
+    def ring_step(hop, k):
         for way in (0, 1):
             if hop >= ring_hops[way]:
                 continue
-            for k in range(2):
-                ring[way, hop, k].wait_recv()
+            ring[way, hop, k].wait_recv()
             if hop + 1 < ring_hops[way]:
-                ring_send_hop(way, hop + 1)
-            for k in range(2):
-                piece = wuv.at[origin(way, hop + 1), core * 2 + k]
-                index = (way * 4 + hop) * 2 + k
-                pair[way, hop, k] = remote(piece, piece, pair_send, pair_recv, index, sibling)
+                ring_hop(way, hop + 1, k)
+            piece = uv_piece(way, hop + 1, k)
+            index = (way * 4 + hop) * 2 + k
+            pair[way, hop, k] = remote(piece, piece, pair_send, pair_recv, index, sibling)
+
+    order = ((0, 1), (-1, 2), (-2, 3), (-3, 4))
+    moved = {}
+
+    def move_half(half):
+        for m, offsets in enumerate(order):
+            for step in (1, 3, 2, 0):
+                to_x = at_x(step)
+                for i, offset in enumerate(offsets):
+                    first = (to_x * NZ + at_z(offset * sign)) * OWN
+                    for p in range(OWN // 2):
+                        for k in range(LAT // LANES):
+                            rows = jnp.concatenate(
+                                [
+                                    lat32[k, pl.ds(half * 8 * HEADS + first + 2 * p + j, 8, stride=HEADS), :]
+                                    for j in range(2)
+                                ],
+                                axis=0,
+                            ).astype(BF16)
+                            where = pl.ds(k * LANES, LANES)
+                            if step == 0:
+                                lat_in[half, m, x, i, p, :, where] = rows
+                            else:
+                                lat_out[half, step - 1, m, i, p, :, where] = rows
+                if step > 0:
+                    moved[half, m, step] = remote(
+                        lat_out.at[half, step - 1, m], lat_in.at[half, m, x], lat_send, lat_recv,
+                        (half * 3 + step - 1) * 4 + m, device(step, 0),
+                    )
+
+    valued = []
+
+    def head_values(m):
+        for half in range(2):
+            for step in range(1, NX):
+                moved[half, m, step].wait_recv()
+        for i, offset in enumerate(order[m]):
+            n = 2 * m + i
+            to_z = at_z(offset * sign)
+            if n > 0:
+                for k in range(2):
+                    pair[(1 if offset < 0 else 0), abs(offset) - 1, k].wait_recv()
+            for p in range(OWN // 2):
+                rows = lat_in[:, m, :, i, p].reshape(2 * NX * SLOTS, LAT)
+                value = jnp.dot(rows, wuv[to_z, p], preferred_element_type=F32)
+                value = value.reshape(2, NX, 2, 8, 2 * VDIM)
+                for row in range(NX):
+                    halves = [
+                        jnp.concatenate([value[h, row, 0, :, :VDIM], value[h, row, 1, :, VDIM:]], axis=1)
+                        for h in range(2)
+                    ]
+                    rows = jnp.concatenate(halves, axis=0).astype(BF16)
+                    at = (pl.ds(row * SLOTS, SLOTS), pl.ds(p * 2 * VDIM, 2 * VDIM))
+                    if n == 0:
+                        hv[z, at[0], at[1]] = rows
+                    else:
+                        hv_out[n - 1, at[0], at[1]] = rows
+            if n > 0:
+                valued.append(
+                    remote(hv_out.at[n - 1], hv.at[z], hv_send, hv_recv, n - 1, device(0, offset * sign))
+                )
 
     attend_groups(0, 1)
     pl.semaphore_wait(barrier, len(peers))
-    uv_load.wait()
-    ring_send_hop(0, 0)
-    ring_send_hop(1, 0)
-    attend_groups(1, 6)
-    ring_step(0)
+    for load in uv_loads:
+        load.wait()
+    for k in range(2):
+        ring_hop(0, 0, k)
+        ring_hop(1, 0, k)
+    attend_groups(1, 4)
+    move_half(0)
+    ring_step(0, 0)
+    attend_groups(4, 6)
+    ring_step(0, 1)
     attend_groups(6, 8)
-
-    order = (0, 1, -1, 2, -2, 3, -3, 4)
-    moved = {}
-    for n, offset in enumerate(order):
-        to_z = at_z(offset * sign)
-        for step in range(NX):
-            to_x = at_x(step)
-
-            @pl.loop(0, OWN, unroll=True)
-            def _(j):
-                head = (to_x * NZ + to_z) * OWN + j
-                for k in range(LAT // LANES):
-                    rows = lat32[k, pl.ds(head, SLOTS, stride=HEADS), :].astype(BF16)
-                    where = pl.ds(k * LANES, LANES)
-                    if step == 0:
-                        lat_in[n, j, x, :, where] = rows
-                    else:
-                        lat_out[step - 1, n, j, :, where] = rows
-
-            if step > 0:
-                moved[n, step] = remote(
-                    lat_out.at[step - 1, n], lat_in.at[n, :, x], lat_send, lat_recv,
-                    (step - 1) * NZ + n, device(step, 0),
-                )
-        if n == 3:
-            ring_step(1)
-
-    valued = []
-    for n, offset in enumerate(order):
-        if n == 2:
-            ring_step(2)
-        if n == 4:
-            ring_step(3)
-        to_z = at_z(offset * sign)
-        if n > 0:
-            hop = abs(offset) - 1
-            for k in range(2):
-                pair[(1 if offset < 0 else 0), hop, k].wait_recv()
-        for step in range(1, NX):
-            moved[n, step].wait_recv()
-        out = hv.at[z] if n == 0 else hv_out.at[n - 1]
-        for j in range(OWN):
-            rows = lat_in[n, j].reshape(NX * SLOTS, LAT)
-            value = jnp.dot(rows, wuv[to_z, j], preferred_element_type=F32)
-            out[:, pl.ds(j * VDIM, VDIM)] = value.astype(BF16)
-        if n > 0:
-            valued.append(remote(out, hv.at[z], hv_send, hv_recv, n - 1, device(0, offset * sign)))
+    ring_step(1, 0)
+    move_half(1)
+    ring_step(1, 1)
+    ring_step(2, 0)
+    ring_step(2, 1)
+    head_values(0)
+    ring_step(3, 0)
+    head_values(1)
+    ring_step(3, 1)
+    head_values(2)
+    head_values(3)
     for copy in valued:
         copy.wait_recv()
 
@@ -235,13 +269,6 @@
         for way in (0, 1):
             send(n, phase, way, 0)
 
-    def next_hops(n, phase, hop):
-        along_x, _, kind, _, _ = streams[n]
-        count = hops(NX if along_x == (phase == 0) else NZ, kind)
-        for way in (0, 1):
-            if hop < count[way]:
-                send(n, phase, way, hop)
-
     def arrivals(n, phase):
         along_x, _, kind, _, _ = streams[n]
         count = hops(NX if along_x == (phase == 0) else NZ, kind)
@@ -274,8 +301,8 @@
         hidden = hidden.astype(F32)
         acc[...] += jnp.sum(hidden * hidden, axis=1, keepdims=True)
 
-    acc[...] = jnp.zeros_like(acc)
-    for n, (along_x, i, _, first, width) in enumerate(streams):
+    def multiply(n):
+        along_x, i, _, first, width = streams[n]
         loads[n].wait()
         part = px if along_x else pz
 
@@ -283,38 +310,39 @@
         def _(tile):
             off = pl.multiple_of(tile * COLS, COLS)
             out = jnp.dot(
-                hv[...].reshape(NX * NZ * SLOTS, DEPTH), wo[:, pl.ds(first + off, COLS)], preferred_element_type=F32
+                hv[...].reshape(NX * NZ * SLOTS, DEPTH), wo[:, pl.ds(first + off, COLS)],
+                preferred_element_type=F32,
             )
             part[i, :, :, :, pl.ds(off, COLS)] = out.astype(BF16).reshape(NZ, NX, SLOTS, COLS)
 
         first_hops(n, 0)
 
-    X, Z = (0, 2, 4, 6), (1, 3, 5, 7)
-    plan = [
-        (next_hops, Z[0], 0, 1), (next_hops, X[0], 0, 1), (next_hops, Z[1], 0, 1),
-        (next_hops, Z[2], 0, 1), (next_hops, X[1], 0, 1), (next_hops, Z[3], 0, 1),
-        (next_hops, Z[0], 0, 2), (next_hops, Z[1], 0, 2), (next_hops, X[2], 0, 1),
-        (next_hops, Z[2], 0, 2), (next_hops, Z[3], 0, 2),
-        (turn, X[0]), (next_hops, X[3], 0, 1), (next_hops, Z[0], 0, 3), (next_hops, Z[1], 0, 3),
-        (turn, X[1]), (next_hops, X[0], 1, 1),
-        (next_hops, Z[2], 0, 3), (next_hops, Z[3], 0, 3),
-        (next_hops, X[1], 1, 1), (next_hops, X[0], 1, 2), (turn, Z[0]), (turn, Z[1]),
-        (next_hops, X[1], 1, 2), (next_hops, X[0], 1, 3), (next_hops, X[1], 1, 3),
-        (turn, X[2]), (turn, Z[2]), (turn, Z[3]), (turn, X[3]),
-        (next_hops, Z[0], 1, 1), (next_hops, Z[1], 1, 1),
-        (next_hops, X[2], 1, 1), (next_hops, X[3], 1, 1),
-        (next_hops, Z[2], 1, 1), (next_hops, Z[3], 1, 1),
-        (next_hops, X[2], 1, 2), (next_hops, X[3], 1, 2),
-        (finish, X[0]), (finish, X[1]),
-        (next_hops, X[2], 1, 3), (next_hops, X[3], 1, 3),
-        (finish, Z[0]), (finish, Z[1]), (finish, Z[2]), (finish, Z[3]),
-        (finish, X[2]), (finish, X[3]),
-    ]
-    for act, *rest in plan:
-        act(*rest)
+    acc[...] = jnp.zeros_like(acc)
+    for n in range(8):
+        multiply(n)
+    for step in (
+        (1, 0, 0, 1), (1, 0, 1, 1), (3, 0, 0, 1), (3, 0, 1, 1), (0, 0, 0, 1), (5, 0, 0, 1),
+        (5, 0, 1, 1), (7, 0, 0, 1), (7, 0, 1, 1), (2, 0, 1, 1), (1, 0, 0, 2), (1, 0, 1, 2),
+        (3, 0, 0, 2), (3, 0, 1, 2), (5, 0, 0, 2), (5, 0, 1, 2), (4, 0, 0, 1), (7, 0, 0, 2),
+        (7, 0, 1, 2), (1, 0, 0, 3), (3, 0, 1, 3), (6, 0, 1, 1), (5, 0, 0, 3), (7, 0, 1, 3),
+        (turn, 0), (turn, 1), (turn, 2), (turn, 3), (turn, 5), (turn, 7),
+        (0, 1, 0, 1), (0, 1, 1, 1), (2, 1, 0, 1), (2, 1, 1, 1), (turn, 4), (turn, 6),
+        (0, 1, 0, 2), (0, 1, 1, 2), (2, 1, 0, 2), (2, 1, 1, 2), (1, 1, 0, 1), (3, 1, 1, 1),
+        (5, 1, 0, 1), (7, 1, 1, 1), (4, 1, 0, 1), (4, 1, 1, 1), (6, 1, 0, 1), (6, 1, 1, 1),
+        (finish, 1), (finish, 3), (0, 1, 0, 3), (finish, 5), (finish, 7), (2, 1, 1, 3),
+        (4, 1, 0, 2), (4, 1, 1, 2), (6, 1, 0, 2), (6, 1, 1, 2), (finish, 0), (finish, 2),
+        (4, 1, 0, 3), (6, 1, 1, 3), (finish, 4), (finish, 6),
+    ):
+        if len(step) == 4:
+            send(*step)
+        else:
+            step[0](step[1])
 
     inv = lax.rsqrt(acc[...] * (1.0 / WIDTH) + norm_eps)
-    mlp_ref[...] = (hid_ref[...].astype(F32) * inv * gain_ref[...].astype(F32)).astype(BF16)
+    gain = gain_ref[...].astype(F32)
+    for k in range(WIDTH // LANES):
+        where = pl.ds(k * LANES, LANES)
+        mlp_ref[:, where] = (hid_ref[:, where].astype(F32) * inv * gain[k : k + 1, :]).astype(BF16)
     for copy in started:
         copy.wait_send()
 
@@ -338,9 +366,9 @@
             pltpu.VMEM((SLOTS, CTX, LAT), BF16),
             pltpu.VMEM((SLOTS, ROPE, CTX), BF16),
             pltpu.VMEM((LAT // LANES, SLOTS * HEADS, LANES), F32),
-            pltpu.VMEM((NX - 1, NZ, OWN, SLOTS, LAT), BF16),
-            pltpu.VMEM((NZ, OWN, NX, SLOTS, LAT), BF16),
-            pltpu.VMEM((NZ, OWN, LAT, VDIM), BF16),
+            pltpu.VMEM((2, NX - 1, 4, 2, OWN // 2, SLOTS, LAT), BF16),
+            pltpu.VMEM((2, 4, NX, 2, OWN // 2, SLOTS, LAT), BF16),
+            pltpu.VMEM((NZ, OWN // 2, LAT, 2 * VDIM), BF16),
             pltpu.VMEM((NZ - 1, NX * SLOTS, DEPTH), BF16),
             pltpu.VMEM((NZ, NX * SLOTS, DEPTH), BF16),
             pltpu.VMEM((DEPTH, WIDTH), BF16),
@@ -351,7 +379,7 @@
             pltpu.VMEM((4, 7, NX, SLOTS, ZW), BF16),
             pltpu.VMEM((4, 3, SLOTS, ZW), BF16),
             pltpu.VMEM((SLOTS, 1), F32),
-            dma((4, SLOTS // GROUP)), dma, dma((8,)),
+            dma((4, SLOTS // GROUP)), dma((OWN,)), dma((8,)),
             dma((16,)), dma((16,)), dma((16,)), dma((16,)),
             dma((24,)), dma((24,)), dma((7,)), dma((7,)), dma((80,)), dma((80,)),
         ],
@@ -363,7 +391,7 @@
         ),
     )(
         q_latent, q_rope, cache_latent, rope_keys, w_uv, w_o, lengths, counts, residual,
-        norm_gain.reshape(1, WIDTH),
+        norm_gain.reshape(WIDTH // LANES, LANES),
     )
     return tuple(outs)
 

time: 122 us -> 111 us (0.910)
  Pallas kernels: 115 us -> 105 us
  local copies, waits for them, and re-layouts: 4.62 us -> 3.28 us
    pallas_call x1, Pallas kernels: 115 us -> 105 us  [body(): pl.pallas_call(decode_kernel, out_shape=[jax.ShapeDtypeStruct((SLOTS, WID...]
    reshape x1 -> x0, local copies, waits for them, and re-layouts: 1.34 us -> none  [body(): norm_gain.reshape(1, WIDTH)]
where the time goes in v3:
time: 111 us; the launch traced here: 110 us
  Pallas kernels  105 us (95%)
  local copies, waits for them, and re-layouts  3.28 us (3%)
  between operations  1.29 us (1%)
    pallas_call x1, Pallas kernels, body(): pl.pallas_call(decode_kernel, out_shape=[jax.ShapeDtypeStruct((SLOTS, WID...  105 us
    unnamed x2, local copies, waits for them, and re-layouts  3.28 us

profile of v3, /device:TPU:32, one launch (start us, length us, event | category | flops | bytes accessed | tf_op | source)
XLA Modules:
  0.0 109.7 jit_solution(16129429570764063801)
XLA Ops:
  1.3 105.1 %shard_map.113 = (bf16[16,7168]{1,0:T(8,128)(2,1)}, bf16[16,7168]{1,0:T(8,128)(2,1)}) custom-call(bf16[16,128,512]{2,1,0:T(8,128)(2,1)} %q_hbm.1, bf16[16,64,128]{2,1,0:T(8,128)(2,1)} %qr_hbm.1, bf16[16,512,512]{2,1,0:T(8,128)(2,1)} %cache_hbm.1, bf16[16,64,512]{2,1,0:T(8,128)(2,1)} %rope_hbm.1, bf16[4,512,128]{2,1,0:T(8,128)(2,1)} %wuv_hbm.1, ...), custom_call_target="tpu_custom_call" | custom-call | flops 3758096384 | bytes 20971520 | tf_op jit(solution)/shard_map/pallas_call | solution.py:358
  106.4 1.6 %copy.15 = bf16[16,7168]{1,0:T(8,128)(2,1)} copy(bf16[16,7168]{1,0:T(8,128)(2,1)} %get-tuple-element.4) | data formatting | bytes 458752
  108.1 1.6 %copy.16 = bf16[16,7168]{1,0:T(8,128)(2,1)} copy(bf16[16,7168]{1,0:T(8,128)(2,1)} %get-tuple-element.5) | data formatting | bytes 458752

commit v4 on v3

--- a/solution.py
+++ b/solution.py
@@ -9,14 +9,14 @@
 log2_e = 1.4426950408889634
 norm_eps = 1e-06
 
-NX, NZ = 4, 8
+NX, NY, NZ = 4, 4, 8
 SLOTS = 16
 HEADS, LAT, VDIM, ROPE, CTX = 128, 512, 128, 64, 512
 OWN = 4
 WIDTH = 7168
 DEPTH = OWN * VDIM
 COLS = 256
-GROUP = 2
+GROUP = 4
 LANES = 128
 XW, ZW = 1024, 768
 MESH = pl.DeviceIdType.MESH
@@ -29,18 +29,22 @@
 
 
 def decode_kernel(
-    q_hbm, qr_hbm, cache_hbm, rope_hbm, wuv_hbm, wo_hbm, lengths_ref, counts_ref, res_ref, gain_ref,
+    q_hbm, qr_hbm, cache_hbm, rope_hbm, wuv_hbm, wo_hbm, res_hbm, gain_hbm, lengths_ref, counts_ref,
     hid_ref, mlp_ref,
-    q_ref, qr_ref, cache_ref, rope_ref, lat32, lat_out, lat_in, wuv, hv_out, hv,
+    res_ref, gain_ref, q_ref, qr_ref, cache_ref, rope_ref, lat32, lat_out, lat_in, wuv, hv_out, hv,
     wo, px, pz, rx1, rx2, rz1, rz2, acc,
-    slot_sem, uv_sem, load_sem,
-    ring_send, ring_recv, pair_send, pair_recv, lat_send, lat_recv, hv_send, hv_recv, send_sem, recv_sem,
+    row_sem, slot_sem, uv_sem, load_sem,
+    ring_send, ring_recv, cross_send, cross_recv, pair_send, pair_recv, lat_send, lat_recv, hv_send, hv_recv, send_sem, recv_sem,
 ):
     dp, grp = lax.axis_index("dp"), lax.axis_index("grp")
     x, z = dp // NZ, dp % NZ
-    core = grp % 2
+    y, core = grp // 2, grp % 2
     sign = 1 - 2 * core
     sibling = (dp, grp + sign)
+    y_pair = y % 2
+
+    def plane(step):
+        return (dp, (y + step + NY) % NY * 2 + core)
 
     def at_x(step):
         return (x + step + NX) % NX
@@ -63,18 +67,10 @@
         return copy
 
     barrier = pltpu.get_barrier_semaphore()
-    peers = [device(d, 0) for d in range(1, NX)] + [device(0, d) for d in range(1, NZ)] + [sibling]
+    peers = [device(d, 0) for d in range(1, NX)] + [device(0, d) for d in range(1, NZ)]
+    peers += [sibling, plane(1), plane(-1)]
     for peer in peers:
         pl.semaphore_signal(barrier, inc=1, device_id=peer, device_id_type=MESH)
-
-    uv_loads = [
-        pltpu.make_async_copy(
-            wuv_hbm.at[j], wuv.at[z, j // 2, :, pl.ds(j % 2 * VDIM, VDIM)], uv_sem.at[j]
-        )
-        for j in range(OWN)
-    ]
-    for load in uv_loads:
-        load.start()
 
     def slot_loads(group):
         where = pl.ds(group * GROUP, GROUP)
@@ -85,9 +81,25 @@
             )
         ]
 
-    for group in range(SLOTS // GROUP):
+    for load in slot_loads(0):
+        load.start()
+    uv_loads = [
+        pltpu.make_async_copy(
+            wuv_hbm.at[j], wuv.at[z, j // 2, :, pl.ds(j % 2 * VDIM, VDIM)], uv_sem.at[j]
+        )
+        for j in range(OWN)
+    ]
+    for load in uv_loads:
+        load.start()
+    for group in range(1, SLOTS // GROUP):
         for load in slot_loads(group):
             load.start()
+    row_loads = [
+        pltpu.make_async_copy(res_hbm, res_ref, row_sem.at[0]),
+        pltpu.make_async_copy(gain_hbm, gain_ref, row_sem.at[1]),
+    ]
+    for load in row_loads:
+        load.start()
 
     streams = []
     for i in range(4):
@@ -103,17 +115,21 @@
 
     position = lax.broadcasted_iota(jnp.int32, (1, CTX), 1)
 
-    def attend(slot):
+    def score(slot):
         scores = lax.dot_general(
             q_ref[slot], cache_ref[slot], (((1,), (1,)), ((), ())), preferred_element_type=F32
         )
         scores += lax.dot_general(
             qr_ref[slot], rope_ref[slot], (((0,), (0,)), ((), ())), preferred_element_type=F32
         )
-        scores = jnp.where(position < lengths_ref[slot], scores, -1e30)
+        return jnp.where(position < lengths_ref[slot], scores, -1e30)
+
+    def soften(scores):
         top = jnp.max(scores, axis=1, keepdims=True)
         expos = jnp.exp2((scores - top) * (score_scale * log2_e))
-        probs = (expos * (1.0 / jnp.sum(expos, axis=1, keepdims=True))).astype(BF16)
+        return (expos * (1.0 / jnp.sum(expos, axis=1, keepdims=True))).astype(BF16)
+
+    def gather(slot, probs):
         rows = pl.ds(pl.multiple_of(slot * HEADS, HEADS), HEADS)
         latents = jnp.dot(probs, cache_ref[slot], preferred_element_type=F32)
         for k in range(LAT // LANES):
@@ -124,34 +140,47 @@
         def _(group):
             for load in slot_loads(group):
                 load.wait()
+            first = group * GROUP
+            scores = [score(first)]
             for j in range(GROUP):
-                attend(group * GROUP + j)
+                if j + 1 < GROUP:
+                    scores.append(score(first + j + 1))
+                gather(first + j, soften(scores[j]))
 
     ring_hops = (NZ // 2, NZ // 2 - 1)
-    ring, pair = {}, {}
-
-    def uv_piece(way, hop, k):
+    ring, pair, cross, cross_pair = {}, {}, {}, {}
+
+    def uv_piece(way, hop, which):
         origin = at_z(hop * (-sign if way == 0 else sign))
-        return wuv.at[origin, core, pl.ds(k * (LAT // 2), LAT // 2)]
-
-    def ring_hop(way, hop, k):
+        return wuv.at[origin, which, pl.ds(pl.multiple_of(core * (LAT // 2), LAT // 2), LAT // 2)]
+
+    def ring_hop(way, hop):
         to = (x * NZ + at_z(sign if way == 0 else -sign), grp)
-        piece = uv_piece(way, hop, k)
-        index = (way * 4 + hop) * 2 + k
-        ring[way, hop, k] = remote(piece, piece, ring_send, ring_recv, index, to)
-
-    def ring_step(hop, k):
+        piece = uv_piece(way, hop, y_pair)
+        ring[way, hop] = remote(piece, piece, ring_send, ring_recv, way * 4 + hop, to)
+
+    def ring_step(hop):
         for way in (0, 1):
             if hop >= ring_hops[way]:
                 continue
-            ring[way, hop, k].wait_recv()
+            ring[way, hop].wait_recv()
             if hop + 1 < ring_hops[way]:
-                ring_hop(way, hop + 1, k)
-            piece = uv_piece(way, hop + 1, k)
-            index = (way * 4 + hop) * 2 + k
-            pair[way, hop, k] = remote(piece, piece, pair_send, pair_recv, index, sibling)
-
-    order = ((0, 1), (-1, 2), (-2, 3), (-3, 4))
+                ring_hop(way, hop + 1)
+            piece = uv_piece(way, hop + 1, y_pair)
+            index = way * 4 + hop
+            cross[way, hop] = remote(piece, piece, cross_send, cross_recv, index, plane(sign))
+            pair[way, hop] = remote(piece, piece, pair_send, pair_recv, index, sibling)
+
+    def cross_step(hop):
+        for way in (0, 1):
+            if hop >= ring_hops[way]:
+                continue
+            cross[way, hop].wait_recv()
+            piece = uv_piece(way, hop + 1, 1 - y_pair)
+            index = 8 + way * 4 + hop
+            cross_pair[way, hop] = remote(piece, piece, pair_send, pair_recv, index, sibling)
+
+    order = ((3, -3), (4, 2), (-2, 1), (-1, 0))
     moved = {}
 
     def move_half(half):
@@ -189,9 +218,10 @@
         for i, offset in enumerate(order[m]):
             n = 2 * m + i
             to_z = at_z(offset * sign)
-            if n > 0:
-                for k in range(2):
-                    pair[(1 if offset < 0 else 0), abs(offset) - 1, k].wait_recv()
+            if offset != 0:
+                came = (1 if offset < 0 else 0, abs(offset) - 1)
+                pair[came].wait_recv()
+                cross_pair[came].wait_recv()
             for p in range(OWN // 2):
                 rows = lat_in[:, m, :, i, p].reshape(2 * NX * SLOTS, LAT)
                 value = jnp.dot(rows, wuv[to_z, p], preferred_element_type=F32)
@@ -203,39 +233,37 @@
                     ]
                     rows = jnp.concatenate(halves, axis=0).astype(BF16)
                     at = (pl.ds(row * SLOTS, SLOTS), pl.ds(p * 2 * VDIM, 2 * VDIM))
-                    if n == 0:
+                    if offset == 0:
                         hv[z, at[0], at[1]] = rows
                     else:
-                        hv_out[n - 1, at[0], at[1]] = rows
-            if n > 0:
+                        hv_out[n, at[0], at[1]] = rows
+            if offset != 0:
                 valued.append(
-                    remote(hv_out.at[n - 1], hv.at[z], hv_send, hv_recv, n - 1, device(0, offset * sign))
+                    remote(hv_out.at[n], hv.at[z], hv_send, hv_recv, n, device(0, offset * sign))
                 )
 
     attend_groups(0, 1)
     pl.semaphore_wait(barrier, len(peers))
     for load in uv_loads:
         load.wait()
-    for k in range(2):
-        ring_hop(0, 0, k)
-        ring_hop(1, 0, k)
-    attend_groups(1, 4)
+    ring_hop(0, 0)
+    ring_hop(1, 0)
+    attend_groups(1, 2)
     move_half(0)
-    ring_step(0, 0)
-    attend_groups(4, 6)
-    ring_step(0, 1)
-    attend_groups(6, 8)
-    ring_step(1, 0)
+    attend_groups(2, 3)
+    ring_step(0)
+    attend_groups(3, 4)
     move_half(1)
-    ring_step(1, 1)
-    ring_step(2, 0)
-    ring_step(2, 1)
+    ring_step(1)
+    cross_step(0)
+    ring_step(2)
+    cross_step(1)
+    cross_step(2)
+    ring_step(3)
     head_values(0)
-    ring_step(3, 0)
-    head_values(1)
-    ring_step(3, 1)
-    head_values(2)
-    head_values(3)
+    cross_step(3)
+    for m in range(1, 4):
+        head_values(m)
     for copy in valued:
         copy.wait_recv()
 
@@ -318,6 +346,8 @@
         first_hops(n, 0)
 
     acc[...] = jnp.zeros_like(acc)
+    for load in row_loads:
+        load.wait()
     for n in range(8):
         multiply(n)
     for step in (
@@ -358,9 +388,11 @@
     outs = pl.pallas_call(
         decode_kernel,
         out_shape=[jax.ShapeDtypeStruct((SLOTS, WIDTH), BF16)] * 2,
-        in_specs=[hbm] * 6 + [smem] * 2 + [vmem] * 2,
+        in_specs=[hbm] * 8 + [smem] * 2,
         out_specs=[vmem, vmem],
         scratch_shapes=[
+            pltpu.VMEM((SLOTS, WIDTH), BF16),
+            pltpu.VMEM((WIDTH // LANES, LANES), BF16),
             pltpu.VMEM((SLOTS, HEADS, LAT), BF16),
             pltpu.VMEM((SLOTS, ROPE, HEADS), BF16),
             pltpu.VMEM((SLOTS, CTX, LAT), BF16),
@@ -379,8 +411,8 @@
             pltpu.VMEM((4, 7, NX, SLOTS, ZW), BF16),
             pltpu.VMEM((4, 3, SLOTS, ZW), BF16),
             pltpu.VMEM((SLOTS, 1), F32),
-            dma((4, SLOTS // GROUP)), dma((OWN,)), dma((8,)),
-            dma((16,)), dma((16,)), dma((16,)), dma((16,)),
+            dma((2,)), dma((4, SLOTS // GROUP)), dma((OWN,)), dma((8,)),
+            dma((8,)), dma((8,)), dma((8,)), dma((8,)), dma((16,)), dma((16,)),
             dma((24,)), dma((24,)), dma((7,)), dma((7,)), dma((80,)), dma((80,)),
         ],
         compiler_params=pltpu.CompilerParams(
@@ -390,8 +422,8 @@
             flops=2 * rows * DEPTH * WIDTH, bytes_accessed=20 * 1024 * 1024, transcendentals=0
         ),
     )(
-        q_latent, q_rope, cache_latent, rope_keys, w_uv, w_o, lengths, counts, residual,
-        norm_gain.reshape(WIDTH // LANES, LANES),
+        q_latent, q_rope, cache_latent, rope_keys, w_uv, w_o, residual,
+        norm_gain.reshape(WIDTH // LANES, LANES), lengths, counts,
     )
     return tuple(outs)
 

time: 111 us -> 108 us (0.973)
  Pallas kernels: 105 us -> 103 us
    pallas_call x1, Pallas kernels: 105 us -> 103 us  [body(): pl.pallas_call(decode_kernel, out_shape=[jax.ShapeDtypeStruct((SLOTS, WID...]
where the time goes in v4:
time: 108 us
  Pallas kernels  103 us (95%)
  local copies, waits for them, and re-layouts  3.28 us (3%)
  between operations  1.29 us (1%)
    pallas_call x1, Pallas kernels, body(): pl.pallas_call(decode_kernel, out_shape=[jax.ShapeDtypeStruct((SLOTS, WID...  103 us
    unnamed x2, local copies, waits for them, and re-layouts  3.28 us

profile of v4, /device:TPU:32, one launch (start us, length us, event | category | flops | bytes accessed | tf_op | source)
XLA Modules:
  0.0 107.8 jit_solution(5190617924056416513)
XLA Ops:
  1.3 103.2 %shard_map.113 = (bf16[16,7168]{1,0:T(8,128)(2,1)}, bf16[16,7168]{1,0:T(8,128)(2,1)}) custom-call(bf16[16,128,512]{2,1,0:T(8,128)(2,1)} %q_hbm.1, bf16[16,64,128]{2,1,0:T(8,128)(2,1)} %qr_hbm.1, bf16[16,512,512]{2,1,0:T(8,128)(2,1)} %cache_hbm.1, bf16[16,64,512]{2,1,0:T(8,128)(2,1)} %rope_hbm.1, bf16[4,512,128]{2,1,0:T(8,128)(2,1)} %wuv_hbm.1, ...), custom_call_target="tpu_custom_call" | custom-call | flops 3758096384 | bytes 20971520 | tf_op jit(solution)/shard_map/pallas_call | solution.py:388
  104.5 1.6 %copy.15 = bf16[16,7168]{1,0:T(8,128)(2,1)} copy(bf16[16,7168]{1,0:T(8,128)(2,1)} %get-tuple-element.4) | data formatting | bytes 458752
  106.1 1.6 %copy.16 = bf16[16,7168]{1,0:T(8,128)(2,1)} copy(bf16[16,7168]{1,0:T(8,128)(2,1)} %get-tuple-element.5) | data formatting | bytes 458752

commit v5 on v4

--- a/solution.py
+++ b/solution.py
@@ -81,8 +81,6 @@
             )
         ]
 
-    for load in slot_loads(0):
-        load.start()
     uv_loads = [
         pltpu.make_async_copy(
             wuv_hbm.at[j], wuv.at[z, j // 2, :, pl.ds(j % 2 * VDIM, VDIM)], uv_sem.at[j]
@@ -90,6 +88,8 @@
         for j in range(OWN)
     ]
     for load in uv_loads:
+        load.start()
+    for load in slot_loads(0):
         load.start()
     for group in range(1, SLOTS // GROUP):
         for load in slot_loads(group):
@@ -180,7 +180,7 @@
             index = 8 + way * 4 + hop
             cross_pair[way, hop] = remote(piece, piece, pair_send, pair_recv, index, sibling)
 
-    order = ((3, -3), (4, 2), (-2, 1), (-1, 0))
+    order = ((3, -3), (2, -2), (4, 1), (-1, 0))
     moved = {}
 
     def move_half(half):
@@ -242,27 +242,25 @@
                     remote(hv_out.at[n], hv.at[z], hv_send, hv_recv, n, device(0, offset * sign))
                 )
 
-    attend_groups(0, 1)
     pl.semaphore_wait(barrier, len(peers))
     for load in uv_loads:
         load.wait()
     ring_hop(0, 0)
     ring_hop(1, 0)
-    attend_groups(1, 2)
+    attend_groups(0, 2)
+    ring_step(0)
     move_half(0)
     attend_groups(2, 3)
-    ring_step(0)
+    ring_step(1)
+    cross_step(0)
     attend_groups(3, 4)
     move_half(1)
-    ring_step(1)
-    cross_step(0)
+    cross_step(1)
     ring_step(2)
-    cross_step(1)
     cross_step(2)
     ring_step(3)
-    head_values(0)
     cross_step(3)
-    for m in range(1, 4):
+    for m in range(4):
         head_values(m)
     for copy in valued:
         copy.wait_recv()
@@ -348,20 +346,19 @@
     acc[...] = jnp.zeros_like(acc)
     for load in row_loads:
         load.wait()
-    for n in range(8):
-        multiply(n)
     for step in (
-        (1, 0, 0, 1), (1, 0, 1, 1), (3, 0, 0, 1), (3, 0, 1, 1), (0, 0, 0, 1), (5, 0, 0, 1),
-        (5, 0, 1, 1), (7, 0, 0, 1), (7, 0, 1, 1), (2, 0, 1, 1), (1, 0, 0, 2), (1, 0, 1, 2),
-        (3, 0, 0, 2), (3, 0, 1, 2), (5, 0, 0, 2), (5, 0, 1, 2), (4, 0, 0, 1), (7, 0, 0, 2),
-        (7, 0, 1, 2), (1, 0, 0, 3), (3, 0, 1, 3), (6, 0, 1, 1), (5, 0, 0, 3), (7, 0, 1, 3),
-        (turn, 0), (turn, 1), (turn, 2), (turn, 3), (turn, 5), (turn, 7),
-        (0, 1, 0, 1), (0, 1, 1, 1), (2, 1, 0, 1), (2, 1, 1, 1), (turn, 4), (turn, 6),
-        (0, 1, 0, 2), (0, 1, 1, 2), (2, 1, 0, 2), (2, 1, 1, 2), (1, 1, 0, 1), (3, 1, 1, 1),
-        (5, 1, 0, 1), (7, 1, 1, 1), (4, 1, 0, 1), (4, 1, 1, 1), (6, 1, 0, 1), (6, 1, 1, 1),
-        (finish, 1), (finish, 3), (0, 1, 0, 3), (finish, 5), (finish, 7), (2, 1, 1, 3),
-        (4, 1, 0, 2), (4, 1, 1, 2), (6, 1, 0, 2), (6, 1, 1, 2), (finish, 0), (finish, 2),
-        (4, 1, 0, 3), (6, 1, 1, 3), (finish, 4), (finish, 6),
+        (multiply, 6), (multiply, 7), (multiply, 1), (multiply, 2), (multiply, 5), (multiply, 3),
+        (5, 0, 0, 1), (5, 0, 1, 1), (1, 0, 0, 1), (6, 0, 1, 1), (7, 0, 1, 1), (multiply, 0),
+        (3, 0, 1, 1), (5, 0, 0, 2), (1, 0, 1, 1), (2, 0, 1, 1), (multiply, 4), (3, 0, 0, 1),
+        (3, 0, 1, 2), (5, 0, 0, 3), (7, 0, 0, 1), (7, 0, 1, 2), (1, 0, 1, 2), (1, 0, 0, 2),
+        (0, 0, 0, 1), (5, 0, 1, 2), (7, 0, 0, 2), (turn, 6), (7, 0, 1, 3), (4, 0, 0, 1),
+        (1, 0, 0, 3), (turn, 5), (turn, 0), (3, 0, 0, 2), (6, 1, 1, 1), (6, 1, 0, 1), (3, 0, 1, 3),
+        (turn, 2), (0, 1, 0, 1), (6, 1, 1, 2), (0, 1, 1, 1), (turn, 7), (turn, 4), (turn, 1),
+        (2, 1, 1, 1), (2, 1, 0, 1), (turn, 3), (0, 1, 0, 2), (6, 1, 1, 3), (4, 1, 0, 1),
+        (1, 1, 0, 1), (2, 1, 0, 2), (2, 1, 1, 2), (4, 1, 1, 1), (5, 1, 0, 1), (0, 1, 0, 3),
+        (4, 1, 0, 2), (0, 1, 1, 2), (6, 1, 0, 2), (3, 1, 1, 1), (7, 1, 1, 1), (2, 1, 1, 3),
+        (finish, 1), (4, 1, 1, 2), (4, 1, 0, 3), (finish, 0), (finish, 5), (finish, 7), (finish, 2),
+        (finish, 6), (finish, 3), (finish, 4),
     ):
         if len(step) == 4:
             send(*step)
@@ -416,7 +413,7 @@
             dma((24,)), dma((24,)), dma((7,)), dma((7,)), dma((80,)), dma((80,)),
         ],
         compiler_params=pltpu.CompilerParams(
-            collective_id=0, has_side_effects=True, vmem_limit_bytes=56 * 1024 * 1024
+            collective_id=0, has_side_effects=True, vmem_limit_bytes=52 * 1024 * 1024
         ),
         cost_estimate=pl.CostEstimate(
             flops=2 * rows * DEPTH * WIDTH, bytes_accessed=20 * 1024 * 1024, transcendentals=0

time: 108 us -> 105 us (0.972)
  Pallas kernels: 103 us -> 97.6 us
  local copies, waits for them, and re-layouts: 3.28 us -> 5.67 us
    pallas_call x1, Pallas kernels: 103 us -> 97.6 us  [body(): pl.pallas_call(decode_kernel, out_shape=[jax.ShapeDtypeStruct((SLOTS, WID...]
    unnamed x2 -> x12, local copies, waits for them, and re-layouts: 3.28 us -> 5.67 us
where the time goes in v5:
time: 105 us
  Pallas kernels  97.6 us (93%)
  local copies, waits for them, and re-layouts  5.67 us (5%)
  between operations  1.3 us (1%)
    pallas_call x1, Pallas kernels, body(): pl.pallas_call(decode_kernel, out_shape=[jax.ShapeDtypeStruct((SLOTS, WID...  97.6 us
    unnamed x12, local copies, waits for them, and re-layouts  5.67 us

profile of v5, /device:TPU:32, one launch (start us, length us, event | category | flops | bytes accessed | tf_op | source)
XLA Modules:
  0.0 104.6 jit_solution(10384719089039563003)
XLA Ops:
  1.3 0.0 copy-start
  1.3 1.0 copy-done
  2.3 0.0 copy-start.1
  2.3 0.9 copy-done.1
  3.3 0.0 copy-start.2
  3.3 0.9 copy-done.2
  4.2 0.0 copy-start.3
  4.2 0.7 copy-done.3
  4.9 0.0 copy-start.4
  4.9 0.7 copy-done.4
  5.6 97.6 %shard_map.113 = (bf16[16,7168]{1,0:T(8,128)(2,1)S(1)}, bf16[16,7168]{1,0:T(8,128)(2,1)S(1)}) custom-call(bf16[16,128,512]{2,1,0:T(8,128)(2,1)} %q_hbm.1, bf16[16,64,128]{2,1,0:T(8,128)(2,1)S(1)} %copy-done.1, bf16[16,512,512]{2,1,0:T(8,128)(2,1)} %cache_hbm.1, bf16[16,64,512]{2,1,0:T(8,128)(2,1)} %rope_hbm.1, bf16[4,512,128]{2,1,0:T(8,128)(2,1)S(1)} %copy-done, ...), custom_call_target="tpu_custom_call" | custom-call | flops 3758096384 | bytes 20971520 | tf_op jit(solution)/shard_map/pallas_call | solution.py:385
  103.2 0.7 copy.15
  103.9 0.7 copy.16
Async XLA Ops:
  1.3 1.0 copy-start
  2.3 0.9 copy-start.1
  3.3 0.9 copy-start.2
  4.2 0.7 copy-start.3
  4.9 0.7 copy-start.4

commit v6 on v5

--- a/solution.py
+++ b/solution.py
@@ -81,6 +81,8 @@
             )
         ]
 
+    for load in slot_loads(0):
+        load.start()
     uv_loads = [
         pltpu.make_async_copy(
             wuv_hbm.at[j], wuv.at[z, j // 2, :, pl.ds(j % 2 * VDIM, VDIM)], uv_sem.at[j]
@@ -88,8 +90,6 @@
         for j in range(OWN)
     ]
     for load in uv_loads:
-        load.start()
-    for load in slot_loads(0):
         load.start()
     for group in range(1, SLOTS // GROUP):
         for load in slot_loads(group):
@@ -242,25 +242,27 @@
                     remote(hv_out.at[n], hv.at[z], hv_send, hv_recv, n, device(0, offset * sign))
                 )
 
+    attend_groups(0, 1)
     pl.semaphore_wait(barrier, len(peers))
     for load in uv_loads:
         load.wait()
     ring_hop(0, 0)
     ring_hop(1, 0)
-    attend_groups(0, 2)
-    ring_step(0)
+    attend_groups(1, 2)
     move_half(0)
     attend_groups(2, 3)
+    ring_step(0)
+    attend_groups(3, 4)
+    move_half(1)
     ring_step(1)
     cross_step(0)
-    attend_groups(3, 4)
-    move_half(1)
+    ring_step(2)
     cross_step(1)
-    ring_step(2)
     cross_step(2)
     ring_step(3)
+    head_values(0)
     cross_step(3)
-    for m in range(4):
+    for m in range(1, 4):
         head_values(m)
     for copy in valued:
         copy.wait_recv()

time: 105 us -> 105 us (level)
  no operation moved by 1% of the time
where the time goes in v6:
time: 105 us
  Pallas kernels  97.7 us (93%)
  local copies, waits for them, and re-layouts  5.67 us (5%)
  between operations  1.3 us (1%)
    pallas_call x1, Pallas kernels, body(): pl.pallas_call(decode_kernel, out_shape=[jax.ShapeDtypeStruct((SLOTS, WID...  97.7 us
    unnamed x12, local copies, waits for them, and re-layouts  5.67 us

profile of v6, /device:TPU:32, one launch (start us, length us, event | category | flops | bytes accessed | tf_op | source)
XLA Modules:
  0.0 104.7 jit_solution(6909251286446555993)
XLA Ops:
  1.3 0.0 copy-start
  1.3 1.0 copy-done
  2.3 0.0 copy-start.1
  2.3 0.9 copy-done.1
  3.3 0.0 copy-start.2
  3.3 0.9 copy-done.2
  4.2 0.0 copy-start.3
  4.2 0.7 copy-done.3
  4.9 0.0 copy-start.4
  4.9 0.7 copy-done.4
  5.6 97.7 %shard_map.113 = (bf16[16,7168]{1,0:T(8,128)(2,1)S(1)}, bf16[16,7168]{1,0:T(8,128)(2,1)S(1)}) custom-call(bf16[16,128,512]{2,1,0:T(8,128)(2,1)} %q_hbm.1, bf16[16,64,128]{2,1,0:T(8,128)(2,1)S(1)} %copy-done.1, bf16[16,512,512]{2,1,0:T(8,128)(2,1)} %cache_hbm.1, bf16[16,64,512]{2,1,0:T(8,128)(2,1)} %rope_hbm.1, bf16[4,512,128]{2,1,0:T(8,128)(2,1)S(1)} %copy-done, ...), custom_call_target="tpu_custom_call" | custom-call | flops 3758096384 | bytes 20971520 | tf_op jit(solution)/shard_map/pallas_call | solution.py:387
  103.3 0.7 copy.15
  104.0 0.7 copy.16
Async XLA Ops:
  1.3 1.0 copy-start
  2.3 0.9 copy-start.1
  3.3 0.9 copy-start.2
  4.2 0.7 copy-start.3
  4.9 0.7 copy-start.4
